TPU v7x, 256 devices: a whole 4x4x8 slice. The times are simulated.
256 devices in a mesh: seq: 32 (over y, x, core), head: 4 (over z_lo), grp: 2 (over z_hi).
Axes of the slice: x: 4, y: 4, z: 8 (z_hi: 2, z_lo: 4; z = z_hi * 4 + z_lo), core: 2. Of those that a mesh axis runs over, the one named last changes fastest.
Arguments:
- queries: bfloat16 [32768, 8192], P(('seq', 'grp'), 'head'), may hold values from -6 to 6
- keys: bfloat16 [32768, 1024], P(('seq', 'grp'), 'head'), may hold values from -6 to 6
- values: bfloat16 [32768, 1024], P(('seq', 'grp'), 'head'), may hold values from -10 to 10
- memory_init: float32 [8, 128, 128], P('head'), may hold values from -256 to 256
- norm_init: float32 [8, 128], P('head'), may hold values from 16 to 64
- gate_logits: float32 [64], replicated, may hold values from -2.5 to 2.5
- dec_queries: bfloat16 [512, 3, 8192], P(('seq', 'head', 'grp')), may hold values from -6 to 6
- cache_keys: bfloat16 [512, 512, 1024], P(('seq', 'head', 'grp')), may hold values from -6 to 6
- cache_values: bfloat16 [512, 512, 1024], P(('seq', 'head', 'grp')), may hold values from -6 to 6
- new_keys: bfloat16 [512, 3, 1024], P(('seq', 'head', 'grp')), may hold values from -6 to 6
- new_values: bfloat16 [512, 3, 1024], P(('seq', 'head', 'grp')), may hold values from -6 to 6
- cache_lengths: int32 [512], P(('seq', 'head', 'grp')), may hold values from 2 to 512, as said below
Outputs:
- prefill_out: bfloat16 [32768, 8192], P(('seq', 'grp'), 'head')
- decode_out: bfloat16 [512, 3, 8192], P(('seq', 'head', 'grp'))
Inputs may be any that keep to these rules, and one draw needn't show every extreme that they name: `cache_lengths`: at least one request has exactly 512 live slots.
All inputs are finite; a program needn't handle non-finite values.
Results may differ from a plain program's by a relative error of at most 0.0045.
Values may be sent and summed in bfloat16 or wider, within the bound.
A program may use at most 128 MiB of HBM per device.

v0:
```python
import math

import jax
import jax.numpy as jnp
from jax import lax
from jax.sharding import PartitionSpec as P


def entering(value, axis, join, neutral):
    place = lax.axis_index(axis)
    gathered = jax.tree.map(
        lambda a, kind: lax.all_gather(a.astype(kind), axis), value, (jnp.bfloat16, jnp.bfloat16)
    )
    state = jax.tree.map(lambda a, e: jnp.zeros_like(a) + jnp.asarray(e, a.dtype), value, neutral)

    def one(hop, state):
        return join(
            state,
            jax.tree.map(
                lambda a, own: lax.dynamic_index_in_dim(a, hop, 0, False).astype(own.dtype),
                gathered,
                value,
            ),
        )

    return lax.fori_loop(0, place, one, state)


def feature_map(values_in):
    widened = values_in.astype(jnp.float32)
    return jnp.where(widened > 0, widened + 1.0, jnp.exp(jnp.minimum(widened, 0.0)))


def retrieve(lifted, memory, norm_vec):
    numer = jnp.einsum("...kgd,kde->...kge", lifted, memory, precision=lax.Precision.HIGHEST)
    denom = jnp.einsum("...kgd,kd->...kg", lifted, norm_vec, precision=lax.Precision.HIGHEST)
    return numer / denom[..., None]


def add_pairs(earlier, later):
    return (earlier[0] + later[0], earlier[1] + later[1])


def on_device(
    queries,
    keys,
    values,
    memory_init,
    norm_init,
    gate_logits,
    dec_queries,
    cache_keys,
    cache_values,
    new_keys,
    new_values,
    cache_lengths,
):
    head_width = memory_init.shape[1]
    key_heads = memory_init.shape[0]
    rows = queries.shape[0]
    query_heads = queries.shape[1] // head_width
    group = query_heads // key_heads
    scale = 1.0 / math.sqrt(head_width)
    half_index = lax.axis_index("grp")
    head_index = lax.axis_index("head")
    all_gates = jax.nn.sigmoid(gate_logits)
    local_gates = lax.dynamic_slice_in_dim(
        all_gates, head_index * query_heads, query_heads
    ).reshape(key_heads, group)[:, :, None]
    paired_keys, paired_values = (
        lax.all_gather(keys, "grp", axis=0, tiled=True),
        lax.all_gather(values, "grp", axis=0, tiled=True),
    )
    prior_keys = paired_keys[:rows]
    prior_values = paired_values[:rows]
    joined_keys = jnp.transpose(
        jnp.concatenate([prior_keys, keys], axis=0).reshape(2 * rows, key_heads, head_width),
        (1, 0, 2),
    )
    joined_values = jnp.transpose(
        jnp.concatenate([prior_values, values], axis=0).reshape(2 * rows, key_heads, head_width),
        (1, 0, 2),
    )
    positions = half_index * rows + jnp.arange(rows)
    key_places = jnp.concatenate([jnp.arange(rows), half_index * rows + jnp.arange(rows)])
    key_usable = jnp.concatenate(
        [jnp.broadcast_to(half_index > 0, (rows,)), jnp.ones((rows,), bool)]
    )
    allowed = (key_places[None, :] <= positions[:, None]) & key_usable[None, :]
    query_major = jnp.transpose(queries.reshape(rows, query_heads, head_width), (1, 0, 2))

    def one_head(items):
        query_one, which = items
        key_one = joined_keys[which]
        value_one = joined_values[which]
        scores = (
            lax.dot_general(
                query_one, key_one, (((1,), (1,)), ((), ())), preferred_element_type=jnp.float32
            )
            * scale
        )
        scores = jnp.where(allowed, scores, -1e30)
        highest = jnp.max(scores, axis=-1, keepdims=True)
        weights = jnp.exp(scores - highest)
        total = jnp.sum(weights, axis=-1, keepdims=True)
        return (
            jnp.dot(weights.astype(jnp.bfloat16), value_one, preferred_element_type=jnp.float32)
            / total
        )

    local = lax.map(one_head, (query_major, jnp.arange(query_heads) // group))
    local = jnp.transpose(local, (1, 0, 2)).reshape(rows, key_heads, group, head_width)
    lifted_keys = feature_map(keys).astype(jnp.bfloat16).reshape(rows, key_heads, head_width)
    own_parts = jnp.einsum(
        "skd,ske->kde",
        lifted_keys,
        values.reshape(rows, key_heads, head_width),
        preferred_element_type=jnp.float32,
    )
    own_sums = jnp.sum(lifted_keys.astype(jnp.float32), axis=0)
    segment_parts, segment_sums = (
        lax.psum(own_parts.astype(jnp.bfloat16), "grp").astype(jnp.float32),
        lax.psum(own_sums.astype(jnp.bfloat16), "grp").astype(jnp.float32),
    )
    zero_parts = jnp.zeros_like(own_parts)
    zero_sums = jnp.zeros_like(own_sums)
    before_parts, before_sums = entering(
        (segment_parts, segment_sums), "seq", add_pairs, (zero_parts, zero_sums)
    )
    through_parts, through_sums = lax.psum((own_parts, own_sums), ("seq", "grp"))
    lifted_queries = feature_map(queries).reshape(rows, key_heads, group, head_width)
    memory_part = retrieve(lifted_queries, memory_init + before_parts, norm_init + before_sums)
    mixed = local_gates * memory_part + (1.0 - local_gates) * local
    prefill_out = mixed.reshape(rows, query_heads * head_width).astype(jnp.bfloat16)
    whole_memory, whole_norm = (
        lax.all_gather(memory_init + through_parts, "head", axis=0, tiled=True),
        lax.all_gather(norm_init + through_sums, "head", axis=0, tiled=True),
    )
    requests = dec_queries.shape[0]
    steps = dec_queries.shape[1]
    slots_count = cache_keys.shape[1]
    every_kv = whole_memory.shape[0]
    every_group = dec_queries.shape[2] // head_width // every_kv
    all_gate_grid = all_gates.reshape(every_kv, every_group)[:, :, None]
    query_grid = dec_queries.reshape(requests, steps, every_kv, every_group, head_width)
    cached_key = cache_keys.reshape(requests, slots_count, every_kv, head_width)
    cached_value = cache_values.reshape(requests, slots_count, every_kv, head_width)
    fresh_key = new_keys.reshape(requests, steps, every_kv, head_width)
    fresh_value = new_values.reshape(requests, steps, every_kv, head_width)
    cache_scores = (
        jnp.einsum("rtkgd,rskd->rkgts", query_grid, cached_key, preferred_element_type=jnp.float32)
        * scale
    )
    live_slots = jnp.arange(slots_count)[None, :] < cache_lengths[:, None]
    cache_scores = jnp.where(live_slots[:, None, None, None, :], cache_scores, -1e30)
    fresh_scores = (
        jnp.einsum("rtkgd,rukd->rkgtu", query_grid, fresh_key, preferred_element_type=jnp.float32)
        * scale
    )
    step_mask = jnp.arange(steps)[:, None] >= jnp.arange(steps)[None, :]
    fresh_scores = jnp.where(step_mask, fresh_scores, -1e30)
    highest = jnp.maximum(jnp.max(cache_scores, axis=-1), jnp.max(fresh_scores, axis=-1))[..., None]
    cache_weights = jnp.exp(cache_scores - highest)
    fresh_weights = jnp.exp(fresh_scores - highest)
    total = jnp.sum(cache_weights, axis=-1) + jnp.sum(fresh_weights, axis=-1)
    dec_local = jnp.einsum(
        "rkgts,rskd->rtkgd",
        cache_weights.astype(jnp.bfloat16),
        cached_value,
        preferred_element_type=jnp.float32,
    )
    dec_local = dec_local + jnp.einsum(
        "rkgtu,rukd->rtkgd",
        fresh_weights.astype(jnp.bfloat16),
        fresh_value,
        preferred_element_type=jnp.float32,
    )
    dec_local = dec_local / jnp.transpose(total, (0, 3, 1, 2))[..., None]
    dec_memory = retrieve(
        feature_map(dec_queries).reshape(requests, steps, every_kv, every_group, head_width),
        whole_memory,
        whole_norm,
    )
    dec_mixed = all_gate_grid * dec_memory + (1.0 - all_gate_grid) * dec_local
    decode_out = dec_mixed.reshape(requests, steps, every_kv * every_group * head_width).astype(
        jnp.bfloat16
    )
    return (prefill_out, decode_out)


def solution(mesh):
    in_specs = (
        P(("seq", "grp"), "head"),
        P(("seq", "grp"), "head"),
        P(("seq", "grp"), "head"),
        P("head", None, None),
        P("head", None),
        P(),
        P(("seq", "head", "grp"), None, None),
        P(("seq", "head", "grp"), None, None),
        P(("seq", "head", "grp"), None, None),
        P(("seq", "head", "grp"), None, None),
        P(("seq", "head", "grp"), None, None),
        P(("seq", "head", "grp")),
    )
    out_specs = (P(("seq", "grp"), "head"), P(("seq", "head", "grp"), None, None))
    return jax.shard_map(
        on_device, mesh=mesh, in_specs=in_specs, out_specs=out_specs, check_vma=False
    )
```

profile of v0, /device:TPU:30, one launch (start us, length us, event | category | flops | bytes accessed | tf_op | source)
XLA Modules:
  0.0 944.0 jit_solution(15928850927278763853)
XLA Ops:
  11.6 19.5 %all_gather.28 = bf16[1024,256]{0,1:T(8,128)(2,1)S(1)} all-gather(bf16[512,256]{0,1:T(8,128)(2,1)S(1)} %copy.58), channel_id=1, replica_groups=mesh['seq'=32,'head'=4,'grp'=2] {'grp'}, dimensions={0}, use_global_device_ids=true | all-gather | bytes 786432 | tf_op jit(solution)/shard_map/all_gather | solution.py:71
  31.2 16.3 %all_gather.29 = bf16[1024,256]{0,1:T(8,128)(2,1)S(1)} all-gather(bf16[512,256]{0,1:T(8,128)(2,1)S(1)} %copy.60), channel_id=1, replica_groups=mesh['seq'=32,'head'=4,'grp'=2] {'grp'}, dimensions={0}, use_global_device_ids=true | all-gather | bytes 786432 | tf_op jit(solution)/shard_map/all_gather | solution.py:72
  48.4 2.5 copy.57
  50.9 93.7 %while.24 = (s32[]{:T(128)}, f32[16,512,128]{2,1,0:T(8,128)}, bf16[16,512,128]{1,2,0:T(8,128)(2,1)}, s32[16]{0:T(128)S(1)}, bf16[2,1024,128]{1,2,0:T(8,128)(2,1)...) while((s32[]{:T(128)}, f32[16,512,128]{2,1,0:T(8,128)}, ...), condition=%wide.region_8.9_spmd.clone, body=%wide.region_5.8_spmd.clone.sunk | while | flops 273218560 | bytes 7227563 | solution.py:111
  53.4 1.6 fusion.99
  59.3 1.6 fusion.99
  65.1 1.6 fusion.99
  67.3 1.2 fusion.101
  71.0 1.6 fusion.99
  73.1 1.2 fusion.101
  76.8 1.6 fusion.99
  79.0 1.2 fusion.101
  82.7 1.6 fusion.99
  84.8 1.2 fusion.101
  88.6 1.6 fusion.99
  90.7 1.2 fusion.101
  94.4 1.6 fusion.99
  96.6 1.2 fusion.101
  100.3 1.6 fusion.99
  102.4 1.2 fusion.101
  106.1 1.6 fusion.99
  108.3 1.2 fusion.101
  112.0 1.6 fusion.99
  114.1 1.2 fusion.101
  117.8 1.6 fusion.99
  120.0 1.2 fusion.101
  123.7 1.6 fusion.99
  129.6 1.6 fusion.99
  135.4 1.6 fusion.99
  141.2 1.6 fusion.99
  143.4 1.2 fusion.101
  145.0 5.4 copy.65
  151.6 2.9 copy.108
  154.5 1.9 copy.109
  156.5 2.2 copy.110
  159.4 1.7 bitcast_bitcast_fusion.1
  162.0 9.4 psum.29
  171.4 195.8 %psum.31 = f32[2,128]{1,0:T(2,128)S(1)} all-reduce(f32[2,128]{1,0:T(2,128)S(1)} %bitcast.182), channel_id=1, replica_groups=mesh['seq'=32,'head'=4,'grp'=2] {'seq','grp'}, use_global_device_ids=true, to_apply=%region_10.11 | all-reduce | flops 256 | bytes 2048 | tf_op jit(solution)/shard_map/psum | solution.py:130
  367.2 27.0 %all_gather.27 = bf16[32,2,128]{2,1,0:T(2,128)(2,1)S(1)} all-gather(bf16[1,2,128]{2,1,0:T(2,128)(2,1)S(1)} %psum.29), channel_id=1, replica_groups=mesh['seq'=32,'head'=4,'grp'=2] {'seq'}, dimensions={0}, use_global_device_ids=true | all-gather | bytes 16896 | tf_op jit(solution)/shard_map/all_gather | solution.py:12
  395.7 374.5 %all-reduce.6.cloned.1.call-done = f32[2,128,128]{2,1,0:T(8,128)} async-done(((f32[2,128,128]{2,1,0:T(8,128)}), f32[2,128,128]{2,1,0:T(8,128)}) %all-reduce.6.cloned.1.call-update) | async-done | bytes 131088 | tf_op jit(solution)/shard_map/psum | solution.py:130
  771.1 15.2 %all_gather.30 = f32[8,128,128]{2,1,0:T(8,128)S(1)} all-gather(f32[2,128,128]{2,1,0:T(8,128)S(1)} %add.109), channel_id=1, replica_groups=mesh['seq'=32,'head'=4,'grp'=2] {'head'}, dimensions={0}, use_global_device_ids=true | all-gather | bytes 655360 | tf_op jit(solution)/shard_map/all_gather | solution.py:136
  786.3 37.8 %all-gather.3.cloned.1.call-done = bf16[32,2,128,128]{3,2,1,0:T(8,128)(2,1)} async-done(((bf16[1,2,128,128]{3,2,1,0:T(8,128)(2,1)}), bf16[32,2,128,128]{3,2,1,0:T(8,128)(2,1)}) %all-gather.3.cloned.1.call-update) | async-done | bytes 2097168 | tf_op jit(solution)/shard_map/all_gather | solution.py:12
  824.2 27.8 %while.23 = (s32[]{:T(128)}, f32[2,128,128]{2,1,0:T(8,128)S(1)}, f32[2,128]{1,0:T(2,128)S(1)}, s32[]{:T(128)}, bf16[32,2,128,128]{3,2,1,0:T(8,128)(2,1)}, /*inde...) while((s32[]{:T(128)}, f32[2,128,128]{2,1,0:T(8,128)S(1)}, f32[2,128]{1,0:T(2,128)S(1)}, ...), condition=%wide.region_4.5_spmd, body=%wide.region_3.4_spmd.sunk | while | flops 66053 | bytes 330375 | solution.py:26
  852.0 57.8 %fusion.22 = f32[2,1,512,8]{3,1,2,0:T(1,128)S(1)} fusion(f32[2,128,1,1]{1,2,3,0:T(1,128)S(1)} %bitcast.181, f32[512,2,8,128]{3,2,1,0:T(8,128)} %bitcast.164), kind=kOutput, calls=%fused_computation.29 | convolution fusion | flops 12582912 | bytes 4228096 | tf_op jit(solution)/shard_map/...kgd,kd->...kg/dot_general | solution.py:36
  910.0 9.8 %fusion.21 = bf16[512,2,8,128]{0,3,2,1:T(8,128)(2,1)S(1)} fusion(f32[512,2,8,128]{0,3,2,1:T(8,128)} %bitcast.168, f32[2,8]{1,0:T(2,128)S(1)} %broadcast_subtract_fusion.1, f32[512,2,8]{0,2,1:T(8,128)S(1)} %bitcast.177, f32[2,8]{1,0:T(2,128)S(1)} %mul.63, f32[512,2,8,128]{3,2,1,0:T(8,128)} %bitcast.165, f32[2,128,128]{2,1,0:T(8,128)S(1)} %copy-done.7, ...), kind=kOutput, calls=%fused_computation.28 | convolution fusion | flops 1615888384 | bytes 10780800 | tf_op jit(solution)/shard_map/...kgd,kde->...kge/dot_general | solution.py:35
  919.8 2.4 copy.77
  922.2 11.1 %all-gather = f32[4,2,128]{2,1,0:T(2,128)S(1)} all-gather(f32[1,2,128]{2,1,0:T(2,128)S(1)} %get-tuple-element.161), channel_id=1, replica_groups=mesh['seq'=32,'head'=4,'grp'=2] {'head'}, dimensions={0}, use_global_device_ids=true | all-gather | bytes 5120 | tf_op jit(solution)/shard_map/all_gather | solution.py:137
  933.3 2.7 fusion.70
  (180 shorter events, 62.4 us)
Async XLA Ops:
  7.2 4.0 copy-start.3
  7.2 4.2 copy-start.4
  7.2 137.6 %all-reduce.4.cloned.1.call-start = ((), (), s32[]{:S(2)}) async-start(), calls=%async_computation | async-start | bytes 131072 | tf_op jit(solution)/shard_map/psum | solution.py:122
  9.7 0.7 copy-start.2
  10.4 759.7 %all-reduce.6.cloned.1.call-start = ((), (), s32[]{:S(2)}) async-start(), calls=%async_computation.2 | async-start | bytes 262144 | tf_op jit(solution)/shard_map/psum | solution.py:130
  11.2 813.0 %all-gather.3.cloned.1.call-start = ((), (), s32[]{:S(2)}) async-start(), calls=%async_computation.1 | async-start | bytes 2162688 | tf_op jit(solution)/shard_map/all_gather | solution.py:12
  31.1 17.3 %copy-start = (bf16[512,2048]{1,0:T(8,128)(2,1)S(1)}, bf16[512,2048]{1,0:T(8,128)(2,1)}, u32[]{:S(2)}) copy-start(bf16[512,2048]{1,0:T(8,128)(2,1)} %param.16) | copy-start | bytes 6291460
  48.4 2.5 copy-start.5
  50.9 93.7 %copy-start.6 = (bf16[2,3,8192]{2,0,1:T(2,128)(2,1)S(1)}, bf16[2,3,8192]{2,0,1:T(2,128)(2,1)}, u32[]{:S(2)}) copy-start(bf16[2,3,8192]{2,0,1:T(2,128)(2,1)} %param.22) | copy-start | bytes 294916
  50.9 93.9 %copy-start.12 = (f32[64]{0:T(128)S(1)}, f32[64]{0:T(128)}, u32[]{:S(2)}) copy-start(f32[64]{0:T(128)} %param.21) | copy-start | bytes 772
  151.5 2.9 copy-start.1
  154.5 1.9 copy-start.8
  154.5 2.0 copy-start.9
  156.5 2.4 copy-start.11
  395.0 375.1 %copy-start.7 = (f32[2,128,128]{2,1,0:T(8,128)S(1)}, f32[2,128,128]{2,1,0:T(8,128)}, u32[]{:S(2)}) copy-start(f32[2,128,128]{2,1,0:T(8,128)} %param.19) | copy-start | bytes 393220
  395.7 456.3 %copy-start.10 = (f32[2,128]{1,0:T(2,128)S(1)}, f32[2,128]{1,0:T(2,128)}, u32[]{:S(2)}) copy-start(f32[2,128]{1,0:T(2,128)} %param.20) | copy-start | bytes 3076
Sparse Core Ops, SparseCore 0:
  11.1 42.9 all-reduce.3
  56.7 713.3 all-reduce.5
  773.0 51.0 all-gather.2
where the time goes:
time: 954 us; the launch traced here: 944 us
  waiting for transfers between devices  413 us (43%)
  blocking collectives  294 us (31%)
  matrix products  120 us (13%)
  other arithmetic  40 us (4%)
  loops' own time  31.5 us (3%)
  local copies, waits for them, and re-layouts  30.7 us (3%)
  between operations  14.4 us (2%)
    psum x1, waiting for transfers between devices, on_device(): lax.psum((own_parts, own_sums), ('seq', 'grp'))  374 us
    psum x1, blocking collectives, on_device(): lax.psum((own_parts, own_sums), ('seq', 'grp'))  196 us
    dot_general x2, matrix products, retrieve(): jnp.einsum('...kgd,kd->...kg', lifted, norm_vec, precision=lax.Precision....  60.4 us
    all_gather x1, waiting for transfers between devices, entering(): lax.all_gather(a.astype(kind), axis)  37.8 us
    another operation x1, loops' own time, on_device(): local = lax.map(one_head, (query_major, jnp.arange(query_heads) // group))  30.2 us
    all_gather x1, blocking collectives, entering(): lax.all_gather(a.astype(kind), axis)  27 us
    add x60, other arithmetic, add_pairs(): return (earlier[0] + later[0], earlier[1] + later[1])  26.4 us
    dot_general x16, matrix products, one_head(): lax.dot_general(query_one, key_one, (((1,), (1,)), ((), ())), preferred_e...  26.2 us
  transfers between devices with their start and end apart: 3, of which 2 were waited for; matrix products, arithmetic and copies ran while one was open for 9% of the time, Pallas kernels for 0%

commit v1 on v0

v1 whole, which is shorter than its diff:
```python
import functools
import math

import jax
import jax.numpy as jnp
from jax import lax
from jax.experimental import pallas as pl
from jax.experimental.pallas import tpu as pltpu
from jax.sharding import PartitionSpec as P

MESH = pl.DeviceIdType.MESH
BF = jnp.bfloat16
F32 = jnp.float32

D = 128
ROWS = 512
G = 8
KH = 2
NK = 8
STEPS = 3
CACHE = 512
OWN = 8
YS = 4
HEADS = 4
SL = D // OWN
B1 = KH * SL + 16
B2 = KH * SL + 8
B4 = KH * D + 16
LOG2E = 1.4426950408889634
C = LOG2E / math.sqrt(D)
NEG = -1e30


def dot(a, b):
    return lax.dot_general(a, b, (((1,), (0,)), ((), ())), preferred_element_type=F32)


def dot_nt(a, b):
    return lax.dot_general(a, b, (((1,), (1,)), ((), ())), preferred_element_type=F32)


def dot_tn(a, b):
    return lax.dot_general(a, b, (((0,), (0,)), ((), ())), preferred_element_type=F32)


def lift(x):
    return jnp.where(x > 0, x + 1.0, jnp.exp(jnp.minimum(x, 0.0)))


def split(x):
    hi = x.astype(BF)
    return hi, (x - hi.astype(F32)).astype(BF)


def inverse(x):
    r = pl.reciprocal(x, approx=True)
    r = r * (2.0 - x * r)
    return r * (2.0 - x * r)


def lanes(s):
    return [s[:, i * D : (i + 1) * D] for i in range(s.shape[1] // D)]


def row_max(tiles):
    top = functools.reduce(jnp.maximum, tiles)
    return jnp.broadcast_to(jnp.max(top, axis=1, keepdims=True), top.shape)


def weights_of(tiles, top):
    shift = top * C
    return jnp.concatenate([jnp.exp2(t * C - shift).astype(BF) for t in tiles], axis=1)


def kernel(
    q_hbm, k_hbm, v_hbm, mem_init, norm_init, gates, dq, ck_hbm, cv_hbm, nk, nv, lengths,
    out_hbm, dec_out,
    q, k, vx, ke, vxe, ck, cv, out,
    acc, den, top, ret,
    gm, gd, qd, nf, fk, fv, dloc,
    snd1, r1, snd2, r2, snd3, r3, snd4, r4, prior, pnorm,
    lsem, osem, kvs, kvr, s1, rs1, s2, rs2, s3, rs3, s4, rs4,
):
    seq = lax.axis_index("seq")
    head = lax.axis_index("head")
    grp = lax.axis_index("grp")
    y = seq // OWN
    o = seq % OWN
    me = grp * OWN + o

    loads = []
    for j in range(KH):
        cols = pl.ds(j * D, D)
        loads.append(pltpu.make_async_copy(k_hbm.at[:, cols], k.at[j], lsem.at[j]))
        loads.append(pltpu.make_async_copy(v_hbm.at[:, cols], vx.at[j, :, 0:D], lsem.at[KH + j]))
    load_q = pltpu.make_async_copy(q_hbm, q, lsem.at[4])
    load_ck = pltpu.make_async_copy(ck_hbm, ck, lsem.at[5])
    load_cv = pltpu.make_async_copy(cv_hbm, cv, lsem.at[6])
    for copy in loads:
        copy.start()
    load_q.start()
    load_ck.start()
    load_cv.start()

    def ring_peer(n):
        t = (me + n) % (2 * OWN)
        return {"seq": y * OWN + t % OWN, "grp": t // OWN}

    def y_peer(n):
        return {"seq": ((y + n) % YS) * OWN + o}

    def head_peer(n):
        return {"head": (head + n) % HEADS}

    barrier = pltpu.get_barrier_semaphore()
    for n in range(1, 2 * OWN):
        pl.semaphore_signal(barrier, inc=1, device_id=ring_peer(n), device_id_type=MESH)
    for n in range(1, YS):
        pl.semaphore_signal(barrier, inc=1, device_id=y_peer(n), device_id_type=MESH)
    for n in range(1, HEADS):
        pl.semaphore_signal(barrier, inc=1, device_id=head_peer(n), device_id_type=MESH)

    for j in range(KH):
        vx[j, :, D:] = jnp.ones((ROWS, D), BF)
        vxe[j, :, D:] = jnp.ones((ROWS, D), BF)
    for copy in loads:
        copy.wait()

    row16 = lax.broadcasted_iota(jnp.int32, (16, D), 0)
    norm_rows = jnp.zeros((16, D), F32)
    for j in range(KH):
        lifted = lift(k[j].astype(F32)).astype(BF)
        part = dot_tn(lifted, vx[j, :, 0:D]).astype(BF)
        for t in range(OWN):
            snd1[t, j * SL : (j + 1) * SL, :] = part[t * SL : (t + 1) * SL]
        norm_rows = norm_rows + jnp.where(
            row16 == j, dot(jnp.ones((16, ROWS), BF), lifted), 0.0
        )
    for t in range(OWN):
        snd1[t, KH * SL :, :] = norm_rows.astype(BF)
    r1[me] = snd1[o]

    pl.semaphore_wait(barrier, 2 * OWN - 1 + YS - 1 + HEADS - 1)

    def send1(n):
        t = (me + n) % (2 * OWN)
        return pltpu.make_async_remote_copy(
            snd1.at[t % OWN], r1.at[me], s1.at[n], rs1.at[n], device_id=ring_peer(n), device_id_type=MESH
        )

    def recv1(n):
        f = (me + 2 * OWN - n) % (2 * OWN)
        return pltpu.make_async_remote_copy(
            snd1.at[o], r1.at[f], s1.at[n], rs1.at[n], device_id=ring_peer(n), device_id_type=MESH
        )

    for n in range(1, 2 * OWN):
        send1(n).start()

    def kv_copy(j, what):
        src, dst = (k.at[j], ke.at[j]) if what == 0 else (vx.at[j, :, 0:D], vxe.at[j, :, 0:D])
        return pltpu.make_async_remote_copy(
            src, dst, kvs.at[2 * j + what], kvr.at[2 * j + what],
            device_id={"grp": 1 - grp}, device_id_type=MESH,
        )

    @pl.when(grp == 0)
    def _():
        for j in range(KH):
            kv_copy(j, 0).start()
            kv_copy(j, 1).start()

    logits = gates[...]
    sig = 1.0 / (1.0 + jnp.exp(-logits))
    at = lax.broadcasted_iota(jnp.int32, (NK * G, NK * G), 0)
    col = lax.broadcasted_iota(jnp.int32, (NK * G, NK * G), 1)
    gm[...] = jnp.broadcast_to(
        jnp.sum(jnp.where(at == col, sig, 0.0), axis=1, keepdims=True), (NK * G, D)
    )
    at = lax.broadcasted_iota(jnp.int32, (NK * G * 4, NK * G), 0)
    col = lax.broadcasted_iota(jnp.int32, (NK * G * 4, NK * G), 1)
    own_row = (at >= col * 4) & (at < col * 4 + 4)
    gd[...] = jnp.broadcast_to(
        jnp.sum(jnp.where(own_row, sig, 0.0), axis=1, keepdims=True), (NK * G * 4, D)
    )

    load_q.wait()

    half = ROWS // 2
    r_at = lax.broadcasted_iota(jnp.int32, (half, D), 0)
    c_at = lax.broadcasted_iota(jnp.int32, (half, D), 1)

    def own_rows(j):
        def one(gi, _):
            h = j * G + gi
            lane = pl.ds(pl.multiple_of(h * D, D), D)
            for b in range(2):
                rows = pl.ds(b * half, half)
                q_one = q[rows, lane]
                tiles = lanes(dot_nt(q_one, k[j, 0 : (b + 1) * half, :]))
                n = len(tiles)
                for i in range(2):
                    keep = c_at + i * D <= r_at
                    tiles[n - 2 + i] = jnp.where(keep, tiles[n - 2 + i], NEG)
                m = row_max(tiles)
                w = weights_of(tiles, m)
                res = dot(w, vx[j, 0 : (b + 1) * half, :])
                acc[h, rows, :] = res[:, :D]
                den[h, rows, :] = res[:, D:]
                top[h, rows, :] = m
            return 0

        lax.fori_loop(0, G, one, 0)

    own_rows(0)

    for n in range(1, 2 * OWN):
        recv1(n).wait_recv()
    run = jnp.zeros((B2, D), F32)
    for t in range(OWN):
        snd3[t, 0:B2, :] = run
        run = run + (r1[t].astype(F32) + r1[OWN + t].astype(F32))[:B2]
    snd2[...] = run
    r2[y] = run

    def send2(n):
        return pltpu.make_async_remote_copy(
            snd2, r2.at[y], s2.at[n], rs2.at[n], device_id=y_peer(n), device_id_type=MESH
        )

    def recv2(n):
        return pltpu.make_async_remote_copy(
            snd2, r2.at[(y + YS - n) % YS], s2.at[n], rs2.at[n], device_id=y_peer(n), device_id_type=MESH
        )

    for n in range(1, YS):
        send2(n).start()

    own_rows(1)

    for n in range(1, YS):
        recv2(n).wait_recv()
    base = jnp.zeros((B2, D), F32)
    total = jnp.zeros((B2, D), F32)
    for t in range(YS):
        base = base + jnp.where(t < y, r2[t], 0.0)
        total = total + r2[t]
    for t in range(OWN):
        snd3[t, 0:B2, :] = snd3[t, 0:B2, :] + base
        snd3[t, B2 : 2 * B2, :] = total
    r3[o] = snd3[o]

    def row_peer(n):
        return {"seq": y * OWN + (o + n) % OWN}

    def send3(n):
        return pltpu.make_async_remote_copy(
            snd3.at[(o + n) % OWN], r3.at[o], s3.at[n], rs3.at[n], device_id=row_peer(n), device_id_type=MESH
        )

    def recv3(n):
        return pltpu.make_async_remote_copy(
            snd3.at[o], r3.at[(o + OWN - n) % OWN], s3.at[n], rs3.at[n],
            device_id=row_peer(n), device_id_type=MESH,
        )

    for n in range(1, OWN):
        send3(n).start()

    qd[...] = jnp.zeros_like(qd)
    fk[...] = jnp.zeros_like(fk)
    fv[...] = jnp.zeros_like(fv)
    nf[...] = jnp.zeros_like(nf)
    for r in range(2):
        for j in range(NK):
            for gi in range(G):
                at_h = (j * G + gi) * D
                qd[r, j, gi * 4 : gi * 4 + STEPS, :] = dq[r, :, at_h : at_h + D].astype(F32)
        nf[0:STEPS, :] = nk[r].astype(F32)
        fk[r, 0:16, :] = nf[...].astype(BF)
        nf[0:STEPS, :] = nv[r].astype(F32)
        fv[r, 0:16, :] = nf[...].astype(BF)
    load_ck.wait()
    load_cv.wait()

    c64 = lax.broadcasted_iota(jnp.int32, (64, D), 1)
    t64 = lax.broadcasted_iota(jnp.int32, (64, D), 0) % 4
    fresh_ok = (c64 <= t64) & (c64 < STEPS)

    def decode(r):
        length = lengths[r]

        def one(p, _):
            lane = pl.ds(pl.multiple_of(p * 2 * D, 2 * D), 2 * D)
            none = jnp.zeros((32, D), BF)
            q0 = qd[r, 2 * p].astype(BF)
            q1 = qd[r, 2 * p + 1].astype(BF)
            both = jnp.concatenate(
                [jnp.concatenate([q0, none], axis=1), jnp.concatenate([none, q1], axis=1)], axis=0
            )
            tiles = lanes(dot_nt(both, ck[r, :, lane]))
            tiles = [jnp.where(c64 + i * D < length, s, NEG) for i, s in enumerate(tiles)]
            tiles.append(jnp.where(fresh_ok, dot_nt(both, fk[r, :, lane]), NEG))
            shift = row_max(tiles) * C
            ws = [jnp.exp2(s * C - shift) for s in tiles]
            tot = jnp.sum(functools.reduce(jnp.add, ws), axis=1, keepdims=True)
            ws = [w.astype(BF) for w in ws]
            res = dot(jnp.concatenate(ws[:-1], axis=1), cv[r, :, lane]) + dot(ws[-1], fv[r, :, lane])
            res = res / tot
            dloc[r, 2 * p] = res[0:32, 0:D]
            dloc[r, 2 * p + 1] = res[32:64, D:]
            return 0

        lax.fori_loop(0, NK // 2, one, 0)

    decode(0)

    for n in range(1, OWN):
        recv3(n).wait_recv()
    for j in range(KH):
        for t in range(OWN):
            at_d = pl.ds(t * SL, SL)
            init = mem_init[j, at_d, :]
            prior[j, at_d, :] = r3[t, j * SL : (j + 1) * SL, :] + init
            snd4[j * D + t * SL : j * D + (t + 1) * SL, :] = (
                r3[t, B2 + j * SL : B2 + (j + 1) * SL, :] + init
            ).astype(BF)
    norms = r3[0, KH * SL : B2, :]
    norms_all = r3[0, B2 + KH * SL : 2 * B2, :]
    row8 = lax.broadcasted_iota(jnp.int32, (8, D), 0)
    init8 = jnp.zeros((8, D), F32)
    for j in range(KH):
        init8 = init8 + jnp.where(row8 == j, norm_init[j : j + 1, :], 0.0)
    pnorm[...] = norms + init8
    snd4[KH * D :, :] = jnp.concatenate([norms_all + init8, jnp.zeros((8, D), F32)], axis=0).astype(BF)
    r4[head] = snd4[...]

    def send4(n):
        return pltpu.make_async_remote_copy(
            snd4, r4.at[head], s4.at[n], rs4.at[n], device_id=head_peer(n), device_id_type=MESH
        )

    def recv4(n):
        return pltpu.make_async_remote_copy(
            snd4, r4.at[(head + HEADS - n) % HEADS], s4.at[n], rs4.at[n],
            device_id=head_peer(n), device_id_type=MESH,
        )

    for n in range(1, HEADS):
        send4(n).start()

    decode(1)

    for j in range(KH):
        m_hi, m_lo = split(prior[j])
        wide = jnp.concatenate([m_hi, m_lo], axis=1)
        numer_w = jnp.concatenate([wide, wide], axis=0)
        n_hi, n_lo = split(jnp.broadcast_to(pnorm[j : j + 1, :], (D, D)))
        tall = jnp.concatenate([n_hi, n_lo], axis=0)
        denom_w = jnp.concatenate([tall, tall], axis=1)

        def one(gi, _, j=j, numer_w=numer_w, denom_w=denom_w):
            h = j * G + gi
            lane = pl.ds(pl.multiple_of(h * D, D), D)
            gate = gm[pl.ds(head * KH * G + h, 1), :]
            for b in range(2):
                rows = pl.ds(b * half, half)
                hi, lo = split(lift(q[rows, lane].astype(F32)))
                pair = jnp.concatenate([hi, lo], axis=1)
                numer = dot(pair, numer_w)
                denom = dot_nt(pair, denom_w)
                ret[h, rows, :] = (
                    (numer[:, :D] + numer[:, D:]) * inverse(denom[:, :D] + denom[:, D:]) * gate
                )
            return 0

        lax.fori_loop(0, G, one, 0)

    for n in range(1, HEADS):
        recv4(n).wait_recv()
    for j in range(NK):
        m_one = r4[j // KH, (j % KH) * D : (j % KH + 1) * D, :]
        numer_w = jnp.concatenate([m_one, m_one], axis=0)
        n_rows = r4[j // KH, KH * D :, :].astype(F32)
        n_one = jnp.broadcast_to(n_rows[j % KH : j % KH + 1, :], (D, D)).astype(BF)
        denom_w = jnp.concatenate([n_one, n_one], axis=1)
        x = jnp.concatenate([qd[0, j], qd[1, j]], axis=0)
        hi, lo = split(lift(x))
        pair = jnp.concatenate([hi, lo], axis=1)
        got = dot(pair, numer_w) * inverse(dot_nt(pair, denom_w))
        gate = gd[j * G * 4 : (j + 1) * G * 4, :]
        for r in range(2):
            mixed = gate * got[r * 32 : (r + 1) * 32] + (1.0 - gate) * dloc[r, j]
            for gi in range(G):
                at_h = (j * G + gi) * D
                dec_out[r, :, at_h : at_h + D] = mixed[gi * 4 : gi * 4 + STEPS].astype(BF)

    def out_copy(j):
        cols = pl.ds(j * G * D, G * D)
        return pltpu.make_async_copy(out.at[:, cols], out_hbm.at[:, cols], osem.at[j])

    def finish(j, later):
        def one(gi, _):
            h = j * G + gi
            lane = pl.ds(pl.multiple_of(h * D, D), D)
            gate = gm[pl.ds(head * KH * G + h, 1), :]
            for b in range(2):
                rows = pl.ds(b * half, half)
                if later:
                    tiles = lanes(dot_nt(q[rows, lane], ke[j]))
                    m_own = top[h, rows, :]
                    m = jnp.maximum(row_max(tiles), m_own)
                    res = dot(weights_of(tiles, m), vxe[j])
                    fade = jnp.exp2((m_own - m) * C)
                    numer = acc[h, rows, :] * fade + res[:, :D]
                    denom = den[h, rows, :] * fade + res[:, D:]
                else:
                    numer = acc[h, rows, :]
                    denom = den[h, rows, :]
                out[rows, lane] = (
                    ret[h, rows, :] + (1.0 - gate) * numer * inverse(denom)
                ).astype(BF)
            return 0

        lax.fori_loop(0, G, one, 0)

    @pl.when(grp == 1)
    def _():
        for j in range(KH):
            kv_copy(j, 0).wait_recv()
            kv_copy(j, 1).wait_recv()
            finish(j, True)
            out_copy(j).start()

    @pl.when(grp == 0)
    def _():
        for j in range(KH):
            finish(j, False)
            out_copy(j).start()
        for j in range(KH):
            kv_copy(j, 0).wait_send()
            kv_copy(j, 1).wait_send()

    for n in range(1, 2 * OWN):
        send1(n).wait_send()
    for n in range(1, YS):
        send2(n).wait_send()
    for n in range(1, OWN):
        send3(n).wait_send()
    for n in range(1, HEADS):
        send4(n).wait_send()
    for j in range(KH):
        out_copy(j).wait()


def on_device(
    queries, keys, values, memory_init, norm_init, gate_logits,
    dec_queries, cache_keys, cache_values, new_keys, new_values, cache_lengths,
):
    hbm = pl.BlockSpec(memory_space=pl.ANY)
    vmem = pl.BlockSpec(memory_space=pltpu.VMEM)
    smem = pl.BlockSpec(memory_space=pltpu.SMEM)
    V = pltpu.VMEM
    DMA = pltpu.SemaphoreType.DMA
    return pl.pallas_call(
        kernel,
        out_shape=(
            jax.ShapeDtypeStruct((ROWS, KH * G * D), BF),
            jax.ShapeDtypeStruct((2, STEPS, NK * G * D), BF),
        ),
        in_specs=[hbm, hbm, hbm, vmem, vmem, vmem, vmem, hbm, hbm, vmem, vmem, smem],
        out_specs=(hbm, vmem),
        scratch_shapes=[
            V((ROWS, KH * G * D), BF),
            V((KH, ROWS, D), BF),
            V((KH, ROWS, 2 * D), BF),
            V((KH, ROWS, D), BF),
            V((KH, ROWS, 2 * D), BF),
            V((2, CACHE, NK * D), BF),
            V((2, CACHE, NK * D), BF),
            V((ROWS, KH * G * D), BF),
            V((KH * G, ROWS, D), F32),
            V((KH * G, ROWS, D), F32),
            V((KH * G, ROWS, D), F32),
            V((KH * G, ROWS, D), F32),
            V((NK * G, D), F32),
            V((NK * G * 4, D), F32),
            V((2, NK, 32, D), F32),
            V((16, NK * D), F32),
            V((2, D, NK * D), BF),
            V((2, D, NK * D), BF),
            V((2, NK, 32, D), F32),
            V((OWN, B1, D), BF),
            V((2 * OWN, B1, D), BF),
            V((B2, D), F32),
            V((YS, B2, D), F32),
            V((OWN, 2 * B2, D), F32),
            V((OWN, 2 * B2, D), F32),
            V((B4, D), BF),
            V((HEADS, B4, D), BF),
            V((KH, D, D), F32),
            V((8, D), F32),
            DMA((7,)), DMA((KH,)), DMA((4,)), DMA((4,)),
            DMA((2 * OWN,)), DMA((2 * OWN,)), DMA((YS,)), DMA((YS,)),
            DMA((OWN,)), DMA((OWN,)), DMA((HEADS,)), DMA((HEADS,)),
        ],
        compiler_params=pltpu.CompilerParams(
            collective_id=0, has_side_effects=True, vmem_limit_bytes=60 * 2**20
        ),
    )(
        queries, keys, values, memory_init, norm_init, gate_logits.reshape(1, -1),
        dec_queries, cache_keys, cache_values, new_keys, new_values, cache_lengths,
    )


def solution(mesh):
    rows = ("seq", "grp")
    every = ("seq", "head", "grp")
    in_specs = (
        P(rows, "head"),
        P(rows, "head"),
        P(rows, "head"),
        P("head", None, None),
        P("head", None),
        P(),
        P(every, None, None),
        P(every, None, None),
        P(every, None, None),
        P(every, None, None),
        P(every, None, None),
        P(every),
    )
    out_specs = (P(rows, "head"), P(every, None, None))
    return jax.shard_map(
        on_device, mesh=mesh, in_specs=in_specs, out_specs=out_specs, check_vma=False
    )
```

time: 954 us -> 71.2 us (0.07)
  the two profiles are of different devices: /device:TPU:30 before, /device:TPU:177 now
where the time goes in v1:
time: 71.2 us; the launch traced here: 70.9 us
  Pallas kernels  61.2 us (86%)
  local copies, waits for them, and re-layouts  9.08 us (13%)
    pallas_call x1, Pallas kernels, on_device(): pl.pallas_call(kernel, out_shape=(jax.ShapeDtypeStruct((ROWS, KH * G * D)...  61.2 us
    unnamed x4, local copies, waits for them, and re-layouts  7.42 us
    pallas_call x1, local copies, waits for them, and re-layouts, on_device(): pl.pallas_call(kernel, out_shape=(jax.ShapeDtypeStruct((ROWS, KH * G * D)...  1.66 us

profile of v1, /device:TPU:177, one launch (start us, length us, event | category | flops | bytes accessed | tf_op | source)
XLA Modules:
  0.0 70.9 jit_solution(3160938375115391633)
XLA Ops:
  0.6 1.3 %copy.15.nk = bf16[2,3,1024]{2,1,0:T(4,128)(2,1)} copy(bf16[2,3,1024]{2,0,1:T(2,128)(2,1)} %param.21) | data formatting | bytes 24576 | tf_op args[9]
  1.9 1.3 %copy.16.nv = bf16[2,3,1024]{2,1,0:T(4,128)(2,1)} copy(bf16[2,3,1024]{2,0,1:T(2,128)(2,1)} %param.22) | data formatting | bytes 24576 | tf_op args[10]
  3.3 1.6 %copy.14.dq = bf16[2,3,8192]{2,1,0:T(4,128)(2,1)} copy(bf16[2,3,8192]{2,0,1:T(2,128)(2,1)} %param.18) | data formatting | bytes 196608 | tf_op args[6]
  4.9 61.2 %shard_map.131 = (bf16[512,2048]{1,0:T(8,128)(2,1)}, bf16[2,3,8192]{2,1,0:T(4,128)(2,1)}) custom-call(bf16[512,2048]{1,0:T(8,128)(2,1)} %q_hbm.1, bf16[512,256]{1,0:T(8,128)(2,1)} %k_hbm.1, bf16[512,256]{1,0:T(8,128)(2,1)} %v_hbm.1, f32[2,128,128]{2,1,0:T(8,128)} %mem_init.1, f32[2,128]{1,0:T(2,128)} %norm_init.1, f32[1,64]{1,0:T(1,128)} %bitcast.1, ...), custom_call_target="tpu_custom_call" | custom-call | tf_op jit(solution)/shard_map/pallas_call | solution.py:465
  66.1 1.7 %copy.17 = bf16[2,3,8192]{2,0,1:T(2,128)(2,1)} copy(bf16[2,3,8192]{2,1,0:T(4,128)(2,1)} %get-tuple-element.3) | data formatting | bytes 196608 | tf_op jit(solution)/shard_map/pallas_call | solution.py:465
  67.7 3.2 %copy.19 = bf16[512,2048]{1,0:T(8,128)(2,1)} copy(bf16[512,2048]{1,0:T(8,128)(2,1)} %get-tuple-element.6) | data formatting | bytes 4194304

commit v2 on v1

v2 whole, which is shorter than its diff:
```python
import functools
import math

import jax
import jax.numpy as jnp
from jax import lax
from jax.experimental import pallas as pl
from jax.experimental.pallas import tpu as pltpu
from jax.sharding import PartitionSpec as P

MESH = pl.DeviceIdType.MESH
BF = jnp.bfloat16
F32 = jnp.float32

D = 128
ROWS = 512
G = 8
KH = 2
NK = 8
STEPS = 3
CACHE = 512
OWN = 8
YS = 4
HEADS = 4
SL = D // OWN
B2 = KH * SL + 8
B4 = KH * D + 16
CHUNKS = 2
CH = ROWS // CHUNKS
AHEAD = 2
UNROLL = 8
LOG2E = 1.4426950408889634
C = LOG2E / math.sqrt(D)
NEG = -1e30


def dot(a, b):
    return lax.dot_general(a, b, (((1,), (0,)), ((), ())), preferred_element_type=F32)


def dot_nt(a, b):
    return lax.dot_general(a, b, (((1,), (1,)), ((), ())), preferred_element_type=F32)


def dot_tn(a, b):
    return lax.dot_general(a, b, (((0,), (0,)), ((), ())), preferred_element_type=F32)


def lift(x):
    return jnp.where(x > 0, x + 1.0, jnp.exp(jnp.minimum(x, 0.0)))


def split(x):
    hi = x.astype(BF)
    return hi, (x - hi.astype(F32)).astype(BF)


def inverse(x):
    r = pl.reciprocal(x, approx=True)
    r = r * (2.0 - x * r)
    return r * (2.0 - x * r)


def lanes(s):
    return [s[:, i * D : (i + 1) * D] for i in range(s.shape[1] // D)]


def row_max(tiles):
    top = functools.reduce(jnp.maximum, tiles)
    return jnp.broadcast_to(jnp.max(top, axis=1, keepdims=True), top.shape)


def weights_of(tiles, top):
    shift = top * C
    return jnp.concatenate([jnp.exp2(t * C - shift).astype(BF) for t in tiles], axis=1)


def each(count, unroll, body):
    def some(i, carry):
        for u in range(unroll):
            body(i * unroll + u)
        return carry

    if count == unroll:
        some(0, 0)
    else:
        lax.fori_loop(0, count // unroll, some, 0)


def kernel(
    q_hbm, k_hbm, v_hbm, mem_init, norm_init, gates, dq, ck_hbm, cv_hbm, nk, nv, lengths,
    out_hbm, dec_out,
    q, kv, kve, ck, cv, out,
    acc, den, top, ret,
    gm, gd, qd, nf, fk, fv, dloc,
    pf, snd0, r0, snd1, r1, snd2, r2, snd3, r3, snd4, r4, r5, prior, pnorm,
    lsem, osem, kvs, kvr, s0, rs0, s1, rs1, s2, rs2, s3, rs3, s4, rs4, s5, rs5,
):
    seq = lax.axis_index("seq")
    head = lax.axis_index("head")
    grp = lax.axis_index("grp")
    y = seq // OWN
    o = seq % OWN

    loads = []
    for j in range(KH):
        cols = pl.ds(j * D, D)
        loads.append(pltpu.make_async_copy(k_hbm.at[:, cols], kv.at[j, :, 0:D], lsem.at[j]))
        loads.append(
            pltpu.make_async_copy(v_hbm.at[:, cols], kv.at[j, :, D : 2 * D], lsem.at[KH + j])
        )
    load_q = pltpu.make_async_copy(q_hbm, q, lsem.at[4])
    load_ck = pltpu.make_async_copy(ck_hbm, ck, lsem.at[5])
    load_cv = pltpu.make_async_copy(cv_hbm, cv, lsem.at[6])
    for copy in loads:
        copy.start()
    load_q.start()
    load_ck.start()
    load_cv.start()

    def grp_peer():
        return {"grp": 1 - grp}

    def row_peer(n):
        return {"seq": y * OWN + (o + n) % OWN}

    def y_peer(n):
        return {"seq": ((y + n) % YS) * OWN + o}

    def head_peer(n):
        return {"head": (head + n) % HEADS}

    peers = [grp_peer()]
    peers += [row_peer(n) for n in range(1, OWN)]
    peers += [y_peer(n) for n in range(1, YS)]
    peers += [head_peer(n) for n in range(1, HEADS)]
    barrier = pltpu.get_barrier_semaphore()
    for peer in peers:
        pl.semaphore_signal(barrier, inc=1, device_id=peer, device_id_type=MESH)

    for j in range(KH):
        kv[j, :, 2 * D :] = jnp.ones((ROWS, D), BF)
        kve[j, :, 2 * D :] = jnp.ones((ROWS, D), BF)
    for copy in loads:
        copy.wait()

    row16 = lax.broadcasted_iota(jnp.int32, (16, D), 0)
    norm_rows = jnp.zeros((16, D), F32)
    for j in range(KH):
        lifted = lift(kv[j, :, 0:D].astype(F32)).astype(BF)
        pf[j * D : (j + 1) * D, :] = dot_tn(lifted, kv[j, :, D : 2 * D])
        norm_rows = norm_rows + jnp.where(
            row16 == j, dot(jnp.ones((16, ROWS), BF), lifted), 0.0
        )
    pf[KH * D :, :] = norm_rows
    snd0[...] = pf[...].astype(BF)

    pl.semaphore_wait(barrier, len(peers))

    def copy0():
        return pltpu.make_async_remote_copy(
            snd0, r0, s0.at[0], rs0.at[0], device_id=grp_peer(), device_id_type=MESH
        )

    copy0().start()

    def kv_copy(c):
        j = c // CHUNKS
        rows = pl.ds(c % CHUNKS * CH, CH)
        return pltpu.make_async_remote_copy(
            kv.at[j, rows, 0 : 2 * D], kve.at[j, rows, 0 : 2 * D], kvs.at[c], kvr.at[c],
            device_id=grp_peer(), device_id_type=MESH,
        )

    def pump(c):
        if c < KH * CHUNKS:

            @pl.when(grp == 0)
            def _():
                kv_copy(c - AHEAD).wait_send()
                kv_copy(c).start()

    def kv_arrived(j, first, last):
        for c in range(j * CHUNKS + first // CH, j * CHUNKS + last // CH):
            kv_copy(c).wait_recv()

    logits = gates[...]
    sig = 1.0 / (1.0 + jnp.exp(-logits))
    at = lax.broadcasted_iota(jnp.int32, (NK * G, NK * G), 0)
    col = lax.broadcasted_iota(jnp.int32, (NK * G, NK * G), 1)
    gm[...] = jnp.broadcast_to(
        jnp.sum(jnp.where(at == col, sig, 0.0), axis=1, keepdims=True), (NK * G, D)
    )
    at = lax.broadcasted_iota(jnp.int32, (NK * G * 4, NK * G), 0)
    col = lax.broadcasted_iota(jnp.int32, (NK * G * 4, NK * G), 1)
    own_row = (at >= col * 4) & (at < col * 4 + 4)
    gd[...] = jnp.broadcast_to(
        jnp.sum(jnp.where(own_row, sig, 0.0), axis=1, keepdims=True), (NK * G * 4, D)
    )

    load_q.wait()

    half = ROWS // 2
    halves = [pl.ds(b * half, half) for b in range(2)]
    r_at = lax.broadcasted_iota(jnp.int32, (half, D), 0)
    c_at = lax.broadcasted_iota(jnp.int32, (half, D), 1)

    def head_lane(h):
        return pl.ds(h * D if isinstance(h, int) else pl.multiple_of(h * D, D), D)

    def own_rows(j):
        def one(gi):
            h = j * G + gi
            queries = [q[rows, head_lane(h)] for rows in halves]
            results = []
            for b in range(2):
                seen = pl.ds(0, (b + 1) * half)
                tiles = lanes(dot_nt(queries[b], kv[j, seen, 0:D]))
                n = len(tiles)
                for i in range(2):
                    tiles[n - 2 + i] = jnp.where(c_at + i * D <= r_at, tiles[n - 2 + i], NEG)
                m = row_max(tiles)
                results.append((m, dot(weights_of(tiles, m), kv[j, seen, D:])))
            for rows, (m, res) in zip(halves, results):
                acc[h, rows, :] = res[:, :D]
                den[h, rows, :] = res[:, D:]
                top[h, rows, :] = m

        each(G, UNROLL, one)

    def square(j, first, last, store):
        seen = pl.ds(first, last - first)

        def one(gi):
            h = j * G + gi
            queries = [q[rows, head_lane(h)] for rows in halves]
            tops = [top[h, rows, :] for rows in halves]
            results = []
            for b in range(2):
                tiles = lanes(dot_nt(queries[b], kve[j, seen, 0:D]))
                m = jnp.maximum(row_max(tiles), tops[b])
                res = dot(weights_of(tiles, m), kve[j, seen, D:])
                fade = jnp.exp2((tops[b] - m) * C)
                results.append((m, fade, res))
            results = [
                (m, acc[h, rows, :] * fade + res[:, :D], den[h, rows, :] * fade + res[:, D:])
                for rows, (m, fade, res) in zip(halves, results)
            ]
            store(h, results)

        each(G, UNROLL, one)

    def keep(h, results):
        for rows, (m, numer, denom) in zip(halves, results):
            acc[h, rows, :] = numer
            den[h, rows, :] = denom
            top[h, rows, :] = m

    def gate_of(h):
        return gm[pl.ds(head * KH * G + h, 1), :]

    def finish(h, results):
        gate = gate_of(h)
        parts = [ret[h, rows, :] for rows in halves]
        for rows, part, (m, numer, denom) in zip(halves, parts, results):
            out[rows, head_lane(h)] = (part + (1.0 - gate) * numer * inverse(denom)).astype(BF)

    own_rows(0)

    copy0().wait_send()

    @pl.when(grp == 0)
    def _():
        for c in range(AHEAD):
            kv_copy(c).start()


    copy0().wait_recv()
    for t in range(OWN):
        for j in range(KH):
            rows = pl.ds(j * D + t * SL, SL)
            snd1[t, j * SL : (j + 1) * SL, :] = pf[rows, :] + r0[rows, :].astype(F32)
        snd1[t, KH * SL :, :] = (pf[KH * D :, :] + r0[KH * D :, :].astype(F32))[0:8]
    r1[o] = snd1[o]

    def send1(n):
        return pltpu.make_async_remote_copy(
            snd1.at[(o + n) % OWN], r1.at[o], s1.at[n], rs1.at[n], device_id=row_peer(n), device_id_type=MESH
        )

    def recv1(n):
        return pltpu.make_async_remote_copy(
            snd1.at[o], r1.at[(o + OWN - n) % OWN], s1.at[n], rs1.at[n],
            device_id=row_peer(n), device_id_type=MESH,
        )

    for n in range(1, OWN):
        send1(n).start()

    own_rows(1)

    for n in range(1, OWN):
        recv1(n).wait_recv()
    run = jnp.zeros((B2, D), F32)
    for t in range(OWN):
        snd3[t] = run[0 : KH * SL]
        run = run + r1[t]
    snd2[...] = run
    r2[y] = run

    def send2(n):
        return pltpu.make_async_remote_copy(
            snd2, r2.at[y], s2.at[n], rs2.at[n], device_id=y_peer(n), device_id_type=MESH
        )

    def recv2(n):
        return pltpu.make_async_remote_copy(
            snd2, r2.at[(y + YS - n) % YS], s2.at[n], rs2.at[n], device_id=y_peer(n), device_id_type=MESH
        )

    for n in range(1, YS):
        send2(n).start()

    qd[...] = jnp.zeros_like(qd)
    fk[...] = jnp.zeros_like(fk)
    fv[...] = jnp.zeros_like(fv)
    nf[...] = jnp.zeros_like(nf)
    for t in range(STEPS):
        for h in range(NK * G):
            j, gi = divmod(h, G)
            two = dq[t, :, h * D : (h + 1) * D].astype(F32)
            for r in range(2):
                qd[j, r * 32 + gi * 4 + t : r * 32 + gi * 4 + t + 1, :] = two[r : r + 1]
    for fresh, wide in ((nk, fk), (nv, fv)):
        for t in range(STEPS):
            two = fresh[t].astype(F32)
            for r in range(2):
                nf[r, t : t + 1, :] = two[r : r + 1]
        for r in range(2):
            wide[r, 0:16, :] = nf[r].astype(BF)
    load_ck.wait()
    load_cv.wait()

    c64 = lax.broadcasted_iota(jnp.int32, (64, D), 1)
    t64 = lax.broadcasted_iota(jnp.int32, (64, D), 0) % 4
    fresh_ok = (c64 <= t64) & (c64 < STEPS)

    def decode(r):
        length = lengths[r]

        def one(p):
            lane = pl.ds(p * 2 * D, 2 * D)
            none = jnp.zeros((32, D), BF)
            q0 = qd[2 * p, 32 * r : 32 * r + 32, :].astype(BF)
            q1 = qd[2 * p + 1, 32 * r : 32 * r + 32, :].astype(BF)
            both = jnp.concatenate(
                [jnp.concatenate([q0, none], axis=1), jnp.concatenate([none, q1], axis=1)], axis=0
            )
            tiles = lanes(dot_nt(both, ck[r, :, lane]))
            tiles = [jnp.where(c64 + i * D < length, s, NEG) for i, s in enumerate(tiles)]
            tiles.append(jnp.where(fresh_ok, dot_nt(both, fk[r, :, lane]), NEG))
            shift = row_max(tiles) * C
            ws = [jnp.exp2(s * C - shift) for s in tiles]
            tot = jnp.sum(functools.reduce(jnp.add, ws), axis=1, keepdims=True)
            ws = [w.astype(BF) for w in ws]
            res = dot(jnp.concatenate(ws[:-1], axis=1), cv[r, :, lane]) + dot(ws[-1], fv[r, :, lane])
            res = res / tot
            dloc[2 * p, 32 * r : 32 * r + 32, :] = res[0:32, 0:D]
            dloc[2 * p + 1, 32 * r : 32 * r + 32, :] = res[32:64, D:]

        each(NK // 2, NK // 2, one)

    decode(0)
    pump(AHEAD)

    for n in range(1, YS):
        recv2(n).wait_recv()
    base = jnp.zeros((B2, D), F32)
    total = jnp.zeros((B2, D), F32)
    for t in range(YS):
        base = base + jnp.where(t < y, r2[t], 0.0)
        total = total + r2[t]
    for t in range(OWN):
        snd3[t] = snd3[t] + base[0 : KH * SL]
    r3[o] = snd3[o]

    def send3(n):
        return pltpu.make_async_remote_copy(
            snd3.at[(o + n) % OWN], r3.at[o], s3.at[n], rs3.at[n], device_id=row_peer(n), device_id_type=MESH
        )

    def recv3(n):
        return pltpu.make_async_remote_copy(
            snd3.at[o], r3.at[(o + OWN - n) % OWN], s3.at[n], rs3.at[n],
            device_id=row_peer(n), device_id_type=MESH,
        )

    for n in range(1, OWN):
        send3(n).start()

    row8 = lax.broadcasted_iota(jnp.int32, (8, D), 0)
    init8 = jnp.zeros((8, D), F32)
    for j in range(KH):
        init8 = init8 + jnp.where(row8 == j, norm_init[j : j + 1, :], 0.0)
    before = base[KH * SL :] + init8
    for t in range(OWN):
        before = before + jnp.where(t < o, r1[t, KH * SL :, :], 0.0)
    pnorm[...] = before
    for j in range(KH):
        init = mem_init[j, pl.ds(pl.multiple_of(o * SL, SL), SL), :]
        snd4[j * SL : (j + 1) * SL, :] = (total[j * SL : (j + 1) * SL] + init).astype(BF)
    snd4[KH * SL :, :] = jnp.concatenate(
        [total[KH * SL :] + init8, jnp.zeros((8, D), F32)], axis=0
    ).astype(BF)
    r4[head] = snd4[...]

    def send4(n):
        return pltpu.make_async_remote_copy(
            snd4, r4.at[head], s4.at[n], rs4.at[n], device_id=head_peer(n), device_id_type=MESH
        )

    def recv4(n):
        return pltpu.make_async_remote_copy(
            snd4, r4.at[(head + HEADS - n) % HEADS], s4.at[n], rs4.at[n],
            device_id=head_peer(n), device_id_type=MESH,
        )

    for n in range(1, HEADS):
        send4(n).start()

    decode(1)
    pump(AHEAD + 1)

    for n in range(1, OWN):
        recv3(n).wait_recv()
    for j in range(KH):
        for t in range(OWN):
            at_d = pl.ds(t * SL, SL)
            prior[j, at_d, :] = r3[t, j * SL : (j + 1) * SL, :] + mem_init[j, at_d, :]

    def retrieve(j, last):
        m_hi, m_lo = split(prior[j])
        wide = jnp.concatenate([m_hi, m_lo], axis=1)
        numer_w = jnp.concatenate([wide, wide], axis=0)
        n_hi, n_lo = split(jnp.broadcast_to(pnorm[j : j + 1, :], (D, D)))
        tall = jnp.concatenate([n_hi, n_lo], axis=0)
        denom_w = jnp.concatenate([tall, tall], axis=1)

        def one(gi):
            h = j * G + gi
            gate = gate_of(h)
            queries = [q[rows, head_lane(h)] for rows in halves]
            if last:
                local = [(acc[h, rows, :], den[h, rows, :]) for rows in halves]
            results = []
            for b in range(2):
                hi, lo = split(lift(queries[b].astype(F32)))
                pair = jnp.concatenate([hi, lo], axis=1)
                numer = dot(pair, numer_w)
                denom = dot_nt(pair, denom_w)
                got = (numer[:, :D] + numer[:, D:]) * inverse(denom[:, :D] + denom[:, D:]) * gate
                if last:
                    got = got + (1.0 - gate) * local[b][0] * inverse(local[b][1])
                results.append(got)
            for rows, got in zip(halves, results):
                if last:
                    out[rows, head_lane(h)] = got.astype(BF)
                else:
                    ret[h, rows, :] = got

        each(G, UNROLL, one)

    def out_copy(j):
        cols = pl.ds(j * G * D, G * D)
        return pltpu.make_async_copy(out.at[:, cols], out_hbm.at[:, cols], osem.at[j])

    @pl.when(grp == 0)
    def _():
        for j in range(KH):
            retrieve(j, True)
            out_copy(j).start()

    @pl.when(grp == 1)
    def _():
        for j in range(KH):
            retrieve(j, False)

    for n in range(1, HEADS):
        recv4(n).wait_recv()
    r5[o] = r4[:, 0 : KH * SL, :]

    def send5(n):
        return pltpu.make_async_remote_copy(
            r4.at[:, 0 : KH * SL, :], r5.at[o], s5.at[n], rs5.at[n],
            device_id=row_peer(n), device_id_type=MESH,
        )

    def recv5(n):
        return pltpu.make_async_remote_copy(
            r4.at[:, 0 : KH * SL, :], r5.at[(o + OWN - n) % OWN], s5.at[n], rs5.at[n],
            device_id=row_peer(n), device_id_type=MESH,
        )

    for n in range(1, OWN):
        send5(n).start()


    @pl.when(grp == 1)
    def _():
        kv_arrived(0, 0, ROWS)
        square(0, 0, ROWS, finish)
        out_copy(0).start()
        kv_arrived(1, 0, half)
        square(1, 0, half, keep)

    for n in range(1, OWN):
        recv5(n).wait_recv()
    for j in range(NK):
        at_s = (j % KH) * SL
        m_one = jnp.concatenate([r5[t, j // KH, at_s : at_s + SL, :] for t in range(OWN)], axis=0)
        numer_w = jnp.concatenate([m_one, m_one], axis=0)
        n_rows = r4[j // KH, KH * SL :, :].astype(F32)
        n_one = jnp.broadcast_to(n_rows[j % KH : j % KH + 1, :], (D, D)).astype(BF)
        denom_w = jnp.concatenate([n_one, n_one], axis=1)
        hi, lo = split(lift(qd[j]))
        pair = jnp.concatenate([hi, lo], axis=1)
        got = dot(pair, numer_w) * inverse(dot_nt(pair, denom_w))
        gate = gd[j * G * 4 : (j + 1) * G * 4, :]
        gate = jnp.concatenate([gate, gate], axis=0)
        mixed = gate * got + (1.0 - gate) * dloc[j]
        for gi in range(G):
            at_h = (j * G + gi) * D
            for t in range(STEPS):
                row = gi * 4 + t
                dec_out[t, :, at_h : at_h + D] = jnp.concatenate(
                    [mixed[row : row + 1], mixed[32 + row : 33 + row]], axis=0
                ).astype(BF)

    @pl.when(grp == 1)
    def _():
        kv_arrived(1, half, ROWS)
        square(1, half, ROWS, finish)
        out_copy(1).start()

    @pl.when(grp == 0)
    def _():
        for c in range(KH * CHUNKS - AHEAD, KH * CHUNKS):
            kv_copy(c).wait_send()

    for n in range(1, OWN):
        send1(n).wait_send()
    for n in range(1, YS):
        send2(n).wait_send()
    for n in range(1, OWN):
        send3(n).wait_send()
    for n in range(1, HEADS):
        send4(n).wait_send()
    for n in range(1, OWN):
        send5(n).wait_send()
    for j in range(KH):
        out_copy(j).wait()


def on_device(
    queries, keys, values, memory_init, norm_init, gate_logits,
    dec_queries, cache_keys, cache_values, new_keys, new_values, cache_lengths,
):
    hbm = pl.BlockSpec(memory_space=pl.ANY)
    vmem = pl.BlockSpec(memory_space=pltpu.VMEM)
    smem = pl.BlockSpec(memory_space=pltpu.SMEM)
    V = pltpu.VMEM
    DMA = pltpu.SemaphoreType.DMA
    prefill, decoded = pl.pallas_call(
        kernel,
        out_shape=(
            jax.ShapeDtypeStruct((ROWS, KH * G * D), BF),
            jax.ShapeDtypeStruct((STEPS, 2, NK * G * D), BF),
        ),
        in_specs=[hbm, hbm, hbm, vmem, vmem, vmem, vmem, hbm, hbm, vmem, vmem, smem],
        out_specs=(hbm, vmem),
        scratch_shapes=[
            V((ROWS, KH * G * D), BF),
            V((KH, ROWS, 3 * D), BF),
            V((KH, ROWS, 3 * D), BF),
            V((2, CACHE, NK * D), BF),
            V((2, CACHE, NK * D), BF),
            V((ROWS, KH * G * D), BF),
            V((KH * G, ROWS, D), F32),
            V((KH * G, ROWS, D), F32),
            V((KH * G, ROWS, D), F32),
            V((KH * G, ROWS, D), F32),
            V((NK * G, D), F32),
            V((NK * G * 4, D), F32),
            V((NK, 64, D), F32),
            V((2, 16, NK * D), F32),
            V((2, D, NK * D), BF),
            V((2, D, NK * D), BF),
            V((NK, 64, D), F32),
            V((B4, D), F32),
            V((B4, D), BF),
            V((B4, D), BF),
            V((OWN, B2, D), F32),
            V((OWN, B2, D), F32),
            V((B2, D), F32),
            V((YS, B2, D), F32),
            V((OWN, KH * SL, D), F32),
            V((OWN, KH * SL, D), F32),
            V((KH * SL + 16, D), BF),
            V((HEADS, KH * SL + 16, D), BF),
            V((OWN, HEADS, KH * SL, D), BF),
            V((KH, D, D), F32),
            V((8, D), F32),
            DMA((7,)), DMA((KH,)), DMA((KH * CHUNKS,)), DMA((KH * CHUNKS,)), DMA((1,)), DMA((1,)),
            DMA((OWN,)), DMA((OWN,)), DMA((YS,)), DMA((YS,)),
            DMA((OWN,)), DMA((OWN,)), DMA((HEADS,)), DMA((HEADS,)),
            DMA((OWN,)), DMA((OWN,)),
        ],
        compiler_params=pltpu.CompilerParams(
            collective_id=0, has_side_effects=True, vmem_limit_bytes=60 * 2**20
        ),
    )(
        queries, keys, values, memory_init, norm_init, gate_logits.reshape(1, -1),
        dec_queries.transpose(1, 0, 2), cache_keys, cache_values,
        new_keys.transpose(1, 0, 2), new_values.transpose(1, 0, 2), cache_lengths,
    )
    return prefill, decoded.transpose(1, 0, 2)


def solution(mesh):
    rows = ("seq", "grp")
    every = ("seq", "head", "grp")
    in_specs = (
        P(rows, "head"),
        P(rows, "head"),
        P(rows, "head"),
        P("head", None, None),
        P("head", None),
        P(),
        P(every, None, None),
        P(every, None, None),
        P(every, None, None),
        P(every, None, None),
        P(every, None, None),
        P(every),
    )
    out_specs = (P(rows, "head"), P(every, None, None))
    return jax.shard_map(
        on_device, mesh=mesh, in_specs=in_specs, out_specs=out_specs, check_vma=False
    )
```

time: 71.2 us -> 48 us (0.67)
  the two profiles are of different devices: /device:TPU:177 before, /device:TPU:1 now
where the time goes in v2:
time: 48 us; the launch traced here: 47.9 us
  Pallas kernels  43.4 us (90%)
  local copies, waits for them, and re-layouts  3.84 us (8%)
  between operations  0.65 us (1%)
    pallas_call x1, Pallas kernels, on_device(): pl.pallas_call(kernel, out_shape=(jax.ShapeDtypeStruct((ROWS, KH * G * D)...  43.4 us
    unnamed x4, local copies, waits for them, and re-layouts  3.84 us

profile of v2, /device:TPU:1, one launch (start us, length us, event | category | flops | bytes accessed | tf_op | source)
XLA Modules:
  0.0 47.9 jit_solution(15949086331566423818)
XLA Ops:
  0.6 43.4 %shard_map.131 = (bf16[512,2048]{1,0:T(8,128)(2,1)}, bf16[3,2,8192]{2,1,0:T(2,128)(2,1)}) custom-call(bf16[512,2048]{1,0:T(8,128)(2,1)} %q_hbm.1, bf16[512,256]{1,0:T(8,128)(2,1)} %k_hbm.1, bf16[512,256]{1,0:T(8,128)(2,1)} %v_hbm.1, f32[2,128,128]{2,1,0:T(8,128)} %mem_init.1, f32[2,128]{1,0:T(2,128)} %norm_init.1, f32[1,64]{1,0:T(1,128)} %bitcast.9, ...), custom_call_target="tpu_custom_call" | custom-call | tf_op jit(solution)/shard_map/pallas_call | solution.py:573
  44.0 0.0 copy-start
  44.0 3.2 %copy.16 = bf16[512,2048]{1,0:T(8,128)(2,1)} copy(bf16[512,2048]{1,0:T(8,128)(2,1)} %get-tuple-element.8) | data formatting | bytes 4194304
  47.2 0.0 copy-done
  47.2 0.6 %copy.17 = bf16[2,3,8192]{2,0,1:T(2,128)(2,1)} copy(bf16[2,3,8192]{2,0,1:T(2,128)(2,1)S(1)} %bitcast.5) | data formatting | bytes 196608
Async XLA Ops:
  44.0 3.2 %copy-start = (bf16[3,2,8192]{2,1,0:T(2,128)(2,1)S(1)}, bf16[3,2,8192]{2,1,0:T(2,128)(2,1)}, u32[]{:S(2)}) copy-start(bf16[3,2,8192]{2,1,0:T(2,128)(2,1)} %get-tuple-element.5) | copy-start | bytes 294916

commit v3 on v2

--- a/solution.py
+++ b/solution.py
@@ -89,12 +89,12 @@
 
 def kernel(
     q_hbm, k_hbm, v_hbm, mem_init, norm_init, gates, dq, ck_hbm, cv_hbm, nk, nv, lengths,
-    out_hbm, dec_out,
-    q, kv, kve, ck, cv, out,
+    out, dec_out,
+    q, kv, kve, ck, cv,
     acc, den, top, ret,
     gm, gd, qd, nf, fk, fv, dloc,
     pf, snd0, r0, snd1, r1, snd2, r2, snd3, r3, snd4, r4, r5, prior, pnorm,
-    lsem, osem, kvs, kvr, s0, rs0, s1, rs1, s2, rs2, s3, rs3, s4, rs4, s5, rs5,
+    lsem, kvs, kvr, s0, rs0, s1, rs1, s2, rs2, s3, rs3, s4, rs4, s5, rs5,
 ):
     seq = lax.axis_index("seq")
     head = lax.axis_index("head")
@@ -371,7 +371,6 @@
         each(NK // 2, NK // 2, one)
 
     decode(0)
-    pump(AHEAD)
 
     for n in range(1, YS):
         recv2(n).wait_recv()
@@ -427,6 +426,7 @@
 
     for n in range(1, HEADS):
         send4(n).start()
+    pump(AHEAD)
 
     decode(1)
     pump(AHEAD + 1)
@@ -470,15 +470,10 @@
 
         each(G, UNROLL, one)
 
-    def out_copy(j):
-        cols = pl.ds(j * G * D, G * D)
-        return pltpu.make_async_copy(out.at[:, cols], out_hbm.at[:, cols], osem.at[j])
-
     @pl.when(grp == 0)
     def _():
         for j in range(KH):
             retrieve(j, True)
-            out_copy(j).start()
 
     @pl.when(grp == 1)
     def _():
@@ -509,7 +504,6 @@
     def _():
         kv_arrived(0, 0, ROWS)
         square(0, 0, ROWS, finish)
-        out_copy(0).start()
         kv_arrived(1, 0, half)
         square(1, 0, half, keep)
 
@@ -540,7 +534,6 @@
     def _():
         kv_arrived(1, half, ROWS)
         square(1, half, ROWS, finish)
-        out_copy(1).start()
 
     @pl.when(grp == 0)
     def _():
@@ -557,15 +550,13 @@
         send4(n).wait_send()
     for n in range(1, OWN):
         send5(n).wait_send()
-    for j in range(KH):
-        out_copy(j).wait()
 
 
 def on_device(
     queries, keys, values, memory_init, norm_init, gate_logits,
     dec_queries, cache_keys, cache_values, new_keys, new_values, cache_lengths,
 ):
-    hbm = pl.BlockSpec(memory_space=pl.ANY)
+    hbm = pl.BlockSpec(memory_space=pltpu.HBM)
     vmem = pl.BlockSpec(memory_space=pltpu.VMEM)
     smem = pl.BlockSpec(memory_space=pltpu.SMEM)
     V = pltpu.VMEM
@@ -573,18 +564,17 @@
     prefill, decoded = pl.pallas_call(
         kernel,
         out_shape=(
-            jax.ShapeDtypeStruct((ROWS, KH * G * D), BF),
-            jax.ShapeDtypeStruct((STEPS, 2, NK * G * D), BF),
+            V((ROWS, KH * G * D), BF),
+            V((STEPS, 2, NK * G * D), BF),
         ),
         in_specs=[hbm, hbm, hbm, vmem, vmem, vmem, vmem, hbm, hbm, vmem, vmem, smem],
-        out_specs=(hbm, vmem),
+        out_specs=(vmem, vmem),
         scratch_shapes=[
             V((ROWS, KH * G * D), BF),
             V((KH, ROWS, 3 * D), BF),
             V((KH, ROWS, 3 * D), BF),
             V((2, CACHE, NK * D), BF),
             V((2, CACHE, NK * D), BF),
-            V((ROWS, KH * G * D), BF),
             V((KH * G, ROWS, D), F32),
             V((KH * G, ROWS, D), F32),
             V((KH * G, ROWS, D), F32),
@@ -610,13 +600,13 @@
             V((OWN, HEADS, KH * SL, D), BF),
             V((KH, D, D), F32),
             V((8, D), F32),
-            DMA((7,)), DMA((KH,)), DMA((KH * CHUNKS,)), DMA((KH * CHUNKS,)), DMA((1,)), DMA((1,)),
+            DMA((7,)), DMA((KH * CHUNKS,)), DMA((KH * CHUNKS,)), DMA((1,)), DMA((1,)),
             DMA((OWN,)), DMA((OWN,)), DMA((YS,)), DMA((YS,)),
             DMA((OWN,)), DMA((OWN,)), DMA((HEADS,)), DMA((HEADS,)),
             DMA((OWN,)), DMA((OWN,)),
         ],
         compiler_params=pltpu.CompilerParams(
-            collective_id=0, has_side_effects=True, vmem_limit_bytes=60 * 2**20
+            collective_id=0, has_side_effects=True, vmem_limit_bytes=61 * 2**20 + 768 * 2**10
         ),
     )(
         queries, keys, values, memory_init, norm_init, gate_logits.reshape(1, -1),

time: 48 us -> 44 us (0.917)
  the two profiles are of different devices: /device:TPU:1 before, /device:TPU:49 now
where the time goes in v3:
time: 44 us; the launch traced here: 43.9 us
  Pallas kernels  41.3 us (94%)
  local copies, waits for them, and re-layouts  1.96 us (4%)
  between operations  0.64 us (1%)
    pallas_call x1, Pallas kernels, on_device(): pl.pallas_call(kernel, out_shape=(V((ROWS, KH * G * D), BF), V((STEPS, 2,...  41.3 us
    unnamed x2, local copies, waits for them, and re-layouts  1.96 us

profile of v3, /device:TPU:49, one launch (start us, length us, event | category | flops | bytes accessed | tf_op | source)
XLA Modules:
  0.0 43.9 jit_solution(11502425912353327901)
XLA Ops:
  0.6 41.3 %shard_map.131 = (bf16[512,2048]{1,0:T(8,128)(2,1)S(1)}, bf16[3,2,8192]{2,1,0:T(2,128)(2,1)S(1)}) custom-call(bf16[512,2048]{1,0:T(8,128)(2,1)} %q_hbm.1, bf16[512,256]{1,0:T(8,128)(2,1)} %k_hbm.1, bf16[512,256]{1,0:T(8,128)(2,1)} %v_hbm.1, f32[2,128,128]{2,1,0:T(8,128)} %mem_init.1, f32[2,128]{1,0:T(2,128)} %norm_init.1, f32[1,64]{1,0:T(1,128)} %bitcast.9, ...), custom_call_target="tpu_custom_call" | custom-call | tf_op jit(solution)/shard_map/pallas_call | solution.py:564
  41.9 1.3 %copy.16 = bf16[512,2048]{1,0:T(8,128)(2,1)} copy(bf16[512,2048]{1,0:T(8,128)(2,1)S(1)} %get-tuple-element.6) | data formatting | bytes 4194304
  43.2 0.6 %copy.17 = bf16[2,3,8192]{2,0,1:T(2,128)(2,1)} copy(bf16[2,3,8192]{2,0,1:T(2,128)(2,1)S(1)} %bitcast.5) | data formatting | bytes 196608

commit v4 on v3

--- a/solution.py
+++ b/solution.py
@@ -470,8 +470,29 @@
 
         each(G, UNROLL, one)
 
+    def send5(n):
+        return pltpu.make_async_remote_copy(
+            r4.at[:, 0 : KH * SL, :], r5.at[o], s5.at[n], rs5.at[n],
+            device_id=row_peer(n), device_id_type=MESH,
+        )
+
+    def recv5(n):
+        return pltpu.make_async_remote_copy(
+            r4.at[:, 0 : KH * SL, :], r5.at[(o + OWN - n) % OWN], s5.at[n], rs5.at[n],
+            device_id=row_peer(n), device_id_type=MESH,
+        )
+
+    def pass_on():
+        for n in range(1, HEADS):
+            recv4(n).wait_recv()
+        r5[o] = r4[:, 0 : KH * SL, :]
+        for n in range(1, OWN):
+            send5(n).start()
+
+
     @pl.when(grp == 0)
     def _():
+        pass_on()
         for j in range(KH):
             retrieve(j, True)
 
@@ -479,26 +500,7 @@
     def _():
         for j in range(KH):
             retrieve(j, False)
-
-    for n in range(1, HEADS):
-        recv4(n).wait_recv()
-    r5[o] = r4[:, 0 : KH * SL, :]
-
-    def send5(n):
-        return pltpu.make_async_remote_copy(
-            r4.at[:, 0 : KH * SL, :], r5.at[o], s5.at[n], rs5.at[n],
-            device_id=row_peer(n), device_id_type=MESH,
-        )
-
-    def recv5(n):
-        return pltpu.make_async_remote_copy(
-            r4.at[:, 0 : KH * SL, :], r5.at[(o + OWN - n) % OWN], s5.at[n], rs5.at[n],
-            device_id=row_peer(n), device_id_type=MESH,
-        )
-
-    for n in range(1, OWN):
-        send5(n).start()
-
+        pass_on()
 
     @pl.when(grp == 1)
     def _():

time: 44 us -> 42 us (0.955)
  the two profiles are of different devices: /device:TPU:49 before, /device:TPU:1 now
where the time goes in v4:
time: 42 us; the launch traced here: 41.9 us
  Pallas kernels  39.3 us (94%)
  local copies, waits for them, and re-layouts  1.96 us (5%)
  between operations  0.64 us (2%)
    pallas_call x1, Pallas kernels, on_device(): pl.pallas_call(kernel, out_shape=(V((ROWS, KH * G * D), BF), V((STEPS, 2,...  39.3 us
    unnamed x2, local copies, waits for them, and re-layouts  1.96 us

profile of v4, /device:TPU:1, one launch (start us, length us, event | category | flops | bytes accessed | tf_op | source)
XLA Modules:
  0.0 41.9 jit_solution(3944796459834043882)
XLA Ops:
  0.6 39.3 %shard_map.131 = (bf16[512,2048]{1,0:T(8,128)(2,1)S(1)}, bf16[3,2,8192]{2,1,0:T(2,128)(2,1)S(1)}) custom-call(bf16[512,2048]{1,0:T(8,128)(2,1)} %q_hbm.1, bf16[512,256]{1,0:T(8,128)(2,1)} %k_hbm.1, bf16[512,256]{1,0:T(8,128)(2,1)} %v_hbm.1, f32[2,128,128]{2,1,0:T(8,128)} %mem_init.1, f32[2,128]{1,0:T(2,128)} %norm_init.1, f32[1,64]{1,0:T(1,128)} %bitcast.9, ...), custom_call_target="tpu_custom_call" | custom-call | tf_op jit(solution)/shard_map/pallas_call | solution.py:566
  40.0 1.3 %copy.16 = bf16[512,2048]{1,0:T(8,128)(2,1)} copy(bf16[512,2048]{1,0:T(8,128)(2,1)S(1)} %get-tuple-element.6) | data formatting | bytes 4194304
  41.3 0.6 %copy.17 = bf16[2,3,8192]{2,0,1:T(2,128)(2,1)} copy(bf16[2,3,8192]{2,0,1:T(2,128)(2,1)S(1)} %bitcast.5) | data formatting | bytes 196608
